TPU v7x, 32 devices: a whole 2x2x4 slice. The times are simulated.
32 devices in a mesh: pool: 2 (over core), seq: 4 (over y, x), dp: 4 (over z).
Axes of the slice: x: 2, y: 2, z: 4, core: 2. Of those that a mesh axis runs over, the one named last changes fastest.
Arguments:
- starting_latents: bfloat16 [8, 64, 512], P(('pool', 'dp'), None, 'seq'), may hold values from -6 to 6
- noise: bfloat16 [8, 8, 64, 512], P(('pool', 'dp'), None, None, 'seq'), may hold values from -6 to 6
- velocity_matrix: float32 [64, 64], replicated, may hold values from -0.75 to 0.75
- kept_rollout_steps: int32 [8, 2], replicated, may hold values from 1 to 8, as said below
- trainer_group_of: int32 [2, 4], replicated, may hold values from 0 to 3, each once within a row
- video_valid_tokens: int32 [8], replicated, may hold values from 128 to 512, as said below
- block_input_states: bfloat16 [8, 512, 3072], P(('pool', 'dp'), 'seq'), may hold values from -6 to 6
- upstream: bfloat16 [8, 2, 512, 2048], P(('pool', 'dp'), None, 'seq'), may hold values from -0.0625 to 0.0625
- patch_embed_weight: bfloat16 [64, 3072], replicated, may hold values from -0.75 to 0.75
- modulation: float32 [2, 8, 3072], replicated, may hold values from -1.5 to 1.5
- frozen_query_key_value: bfloat16 [3072, 6144], P(('pool', 'dp')), may hold values from -0.109375 to 0.109375
- query_down_factor: bfloat16 [3072, 128], replicated, may hold values from -0.109375 to 0.109375
- query_up_factor: bfloat16 [128, 2048], replicated, may hold values from -0.5 to 0.5
Outputs:
- grad_down: float32 [3072, 128], P('dp')
- grad_up: float32 [128, 2048], P(None, 'dp')
- final_latent: float32 [8, 64, 512], P(('pool', 'dp'), None, 'seq')
Inputs may be any that keep to these rules, and one draw needn't show every extreme that they name: `kept_rollout_steps`: the 2 entries of a row are distinct. `trainer_group_of`: each row names every group once. `video_valid_tokens`: tokens of a video at positions from this count on are padding; some video is full.
All inputs are finite; a program needn't handle non-finite values.
Results may differ from a plain program's by a relative error of at most 0.0088.
Values may be sent and summed in bfloat16 or wider, within the bound.
A program may use at most 128 MiB of HBM per device.

v0:
```python
import math

import jax
import jax.numpy as jnp
from jax import lax
from jax.sharding import PartitionSpec as P

HEADS = 16
HEAD_DIM = 128


epsilon = 1e-06
noise_level = 0.5


def partner(block, axis, apart):
    count = lax.axis_size(axis)
    route = []
    for low in range(count):
        high = low | 1 << apart
        if high != low and high < count:
            route += [(low, high), (high, low)]
    return lax.ppermute(block, axis, route)


def norm_rows(values):
    return values * lax.rsqrt(jnp.mean(values * values, -1, keepdims=True) + epsilon)


def layer_norm(values):
    centered = values - jnp.mean(values, -1, keepdims=True)
    return centered * lax.rsqrt(jnp.mean(centered * centered, -1, keepdims=True) + epsilon)


def norm_backward(raw, grad_normed):
    inverse = lax.rsqrt(jnp.mean(raw * raw, -1, keepdims=True) + epsilon)
    normal = raw * inverse
    gradient = grad_normed.astype(jnp.float32)
    inner_mean = jnp.mean(gradient * normal, -1, keepdims=True)
    return (inverse * (gradient - normal * inner_mean)).astype(jnp.bfloat16)


def rows_product(rows_bf, right):
    upper = right.astype(jnp.bfloat16)
    lower = (right - upper.astype(jnp.float32)).astype(jnp.bfloat16)
    dims = (((0,), (0,)), ((), ()))
    first_part = lax.dot_general(rows_bf, upper, dims, preferred_element_type=jnp.float32)
    return first_part + lax.dot_general(rows_bf, lower, dims, preferred_element_type=jnp.float32)


def attend_head(query, keys, values, gradient_output, token_length):
    total_rows = query.shape[0]
    block_rows = 512
    positions = jnp.arange(total_rows, dtype=jnp.int32)
    key_mask = (positions < token_length).astype(jnp.float32)
    factor = query.shape[1] ** (-0.5)

    def one_block(number):
        begin = number * block_rows
        query_rows = lax.dynamic_slice_in_dim(query, begin, block_rows, 0)
        grad_rows = lax.dynamic_slice_in_dim(gradient_output, begin, block_rows, 0)
        row_mask = (begin + jnp.arange(block_rows, dtype=jnp.int32) < token_length).astype(
            grad_rows.dtype
        )
        grad_rows = grad_rows * row_mask[:, None]
        scores = (
            lax.dot_general(
                query_rows, keys, (((1,), (1,)), ((), ())), preferred_element_type=jnp.float32
            )
            * factor
        )
        weights = jnp.exp(scores) * key_mask[None, :]
        probs = weights / jnp.sum(weights, -1, keepdims=True)
        output = jnp.dot(probs.astype(jnp.bfloat16), values, preferred_element_type=jnp.float32)
        row_delta = jnp.sum(grad_rows.astype(jnp.float32) * output, -1, keepdims=True)
        grad_probs = lax.dot_general(
            grad_rows, values, (((1,), (1,)), ((), ())), preferred_element_type=jnp.float32
        )
        grad_scores = (probs * (grad_probs - row_delta)).astype(jnp.bfloat16)
        return (jnp.dot(grad_scores, keys, preferred_element_type=jnp.float32) * factor).astype(
            jnp.bfloat16
        )

    blocks = lax.map(one_block, jnp.arange(total_rows // block_rows, dtype=jnp.int32))
    return blocks.reshape(total_rows, query.shape[1])


def attend_all(query, keys, values, gradient_output, token_length):
    samples, total_rows, head_count, head_width = query.shape

    def flatten(array):
        return jnp.transpose(array, (0, 2, 1, 3)).reshape(
            samples * head_count, total_rows, head_width
        )

    def per_head(group):
        return attend_head(group[0], group[1], group[2], group[3], token_length)

    result = lax.map(
        per_head, (flatten(query), flatten(keys), flatten(values), flatten(gradient_output))
    )
    return jnp.transpose(result.reshape(samples, head_count, total_rows, head_width), (0, 2, 1, 3))


def body(
    starting_latents,
    noise,
    velocity_matrix,
    kept_rollout_steps,
    trainer_group_of,
    video_valid_tokens,
    block_input_states,
    upstream,
    patch_embed_weight,
    modulation,
    frozen_query_key_value,
    query_down_factor,
    query_up_factor,
):
    halves = lax.axis_size("pool")
    groups = lax.axis_size("dp")
    half = lax.axis_index("pool")
    group = lax.axis_index("dp")
    videos = halves * groups
    video = half * groups + group
    video_ids = jnp.arange(videos, dtype=jnp.int32)
    steps_total = noise.shape[1]
    step_size = 1.0 / steps_total
    own_steps = jnp.sum(jnp.where((video_ids == video)[:, None], kept_rollout_steps, 0), 0)
    state = starting_latents[0].astype(jnp.float32)
    kept_rows = jnp.zeros((own_steps.shape[0],) + state.shape, jnp.float32)
    for step in range(steps_total):
        drift = jnp.dot(velocity_matrix, state, precision=lax.Precision.HIGHEST)
        state = (
            state
            - step_size * drift
            + noise_level * math.sqrt(step_size) * noise[0, step].astype(jnp.float32)
        )
        kept_rows = jnp.where((own_steps == step + 1)[:, None, None], state[None], kept_rows)
    kept_rows = kept_rows.astype(jnp.bfloat16)
    source_half = 1 - half
    trainer_row = jnp.sum(
        jnp.where(
            (jnp.arange(halves, dtype=jnp.int32) == source_half)[:, None], trainer_group_of, 0
        ),
        0,
    )
    source_group = jnp.sum(jnp.where(trainer_row == group, jnp.arange(groups, dtype=jnp.int32), 0))
    source = source_half * groups + source_group
    swapped = partner(kept_rows, "pool", 0)
    spread = lax.all_gather(swapped[None], "dp", axis=0, tiled=True)
    chosen = jnp.arange(groups, dtype=jnp.int32) == source_group
    received = jnp.sum(
        jnp.where(chosen[:, None, None, None], spread.astype(jnp.float32), 0.0), 0
    ).astype(jnp.bfloat16)
    train_steps = jnp.sum(jnp.where((video_ids == source)[:, None], kept_rollout_steps, 0), 0)
    token_length = jnp.sum(jnp.where(video_ids == source, video_valid_tokens, 0))
    embedded = lax.dot_general(
        received, patch_embed_weight, (((1,), (0,)), ((), ())), preferred_element_type=jnp.float32
    )
    hidden = block_input_states[0].astype(jnp.float32)[None] + embedded
    one_hot = (
        train_steps[:, None] - 1 == jnp.arange(steps_total, dtype=jnp.int32)[None, :]
    ).astype(jnp.float32)
    mod_scale = jnp.dot(one_hot, modulation[0], precision=lax.Precision.HIGHEST)
    mod_shift = jnp.dot(one_hot, modulation[1], precision=lax.Precision.HIGHEST)
    normed = (layer_norm(hidden) * (1.0 + mod_scale[:, None, :]) + mod_shift[:, None, :]).astype(
        jnp.bfloat16
    )
    keep_count, tok_rows, width = normed.shape
    inner_width = query_up_factor.shape[1]
    grad_tokens = upstream[0].reshape(keep_count, tok_rows, HEADS, HEAD_DIM)
    flattened_rows = normed.reshape(keep_count * tok_rows, width)
    projected_rows = jnp.dot(
        flattened_rows,
        lax.all_gather(frozen_query_key_value, ("pool", "dp"), axis=0, tiled=True),
        preferred_element_type=jnp.float32,
    )
    lowrank_product = jnp.dot(
        flattened_rows, query_down_factor, preferred_element_type=jnp.float32
    ).astype(jnp.bfloat16)
    query_unscaled = projected_rows[:, :inner_width] + jnp.dot(
        lowrank_product, query_up_factor, preferred_element_type=jnp.float32
    )
    query_unscaled = query_unscaled.reshape(keep_count, tok_rows, HEADS, HEAD_DIM)
    key_raw = projected_rows[:, inner_width : 2 * inner_width].reshape(
        keep_count, tok_rows, HEADS, HEAD_DIM
    )
    value_heads = (
        projected_rows[:, 2 * inner_width :]
        .astype(jnp.bfloat16)
        .reshape(keep_count, tok_rows, HEADS, HEAD_DIM)
    )
    query_heads = norm_rows(query_unscaled).astype(jnp.bfloat16)
    key_heads = norm_rows(key_raw).astype(jnp.bfloat16)
    query_all, key_all, value_all, grad_all = (
        lax.all_to_all(query_heads, "seq", split_axis=2, concat_axis=1, tiled=True),
        lax.all_to_all(key_heads, "seq", split_axis=2, concat_axis=1, tiled=True),
        lax.all_to_all(value_heads, "seq", split_axis=2, concat_axis=1, tiled=True),
        lax.all_to_all(grad_tokens, "seq", split_axis=2, concat_axis=1, tiled=True),
    )
    grad_normed = attend_all(query_all, key_all, value_all, grad_all, token_length)
    grad_local = lax.all_to_all(grad_normed, "seq", split_axis=1, concat_axis=2, tiled=True)
    gradient_query = norm_backward(query_unscaled, grad_local).reshape(
        keep_count * tok_rows, inner_width
    )
    grad_up = jnp.dot(lowrank_product.T, gradient_query, preferred_element_type=jnp.float32)
    gradient_lowrank = jnp.dot(
        gradient_query, query_up_factor.T, preferred_element_type=jnp.float32
    )
    grad_down = rows_product(flattened_rows, gradient_lowrank)
    summed = lax.psum((grad_down, grad_up), ("pool", "seq"))
    owned = (
        lax.psum_scatter(summed[0], "dp", scatter_dimension=0, tiled=True),
        lax.psum_scatter(summed[1], "dp", scatter_dimension=1, tiled=True),
    )
    return (owned[0], owned[1], state[None])


def solution(mesh):
    return jax.shard_map(
        body,
        mesh=mesh,
        in_specs=(
            P(("pool", "dp"), None, "seq"),
            P(("pool", "dp"), None, None, "seq"),
            P(),
            P(),
            P(),
            P(),
            P(("pool", "dp"), "seq", None),
            P(("pool", "dp"), None, "seq", None),
            P(),
            P(),
            P(("pool", "dp"), None),
            P(),
            P(),
        ),
        out_specs=(P("dp", None), P(None, "dp"), P(("pool", "dp"), None, "seq")),
        check_vma=False,
    )
```

profile of v0, /device:TPU:0, one launch (start us, length us, event | category | flops | bytes accessed | tf_op | source)
XLA Modules:
  0.0 634.7 jit_solution(5645922505798686753)
XLA Ops:
  12.3 1.3 copy.102
  13.6 4.9 all-to-all-start.2
  19.8 14.1 %all-gather = bf16[8,64,128]{2,1,0:T(8,128)(2,1)S(1)} all-gather(bf16[2,64,128]{2,1,0:T(8,128)(2,1)S(1)} %collective-permute-done), channel_id=2, replica_groups=mesh['pool'=2,'seq'=4,'dp'=4] {'dp'}, dimensions={0}, use_global_device_ids=true | all-gather | bytes 163840 | tf_op jit(solution)/shard_map/all_gather | solution.py:151
  36.5 301.3 %all-gather.3.cloned.1.call-done = bf16[3072,6144]{1,0:T(8,128)(2,1)} async-done(((bf16[384,6144]{1,0:T(8,128)(2,1)}), bf16[3072,6144]{1,0:T(8,128)(2,1)}) %all-gather.3.cloned.1.call-update) | async-done | bytes 37748752 | tf_op jit(solution)/shard_map/all_gather | solution.py:176
  337.8 18.7 %fusion.85 = f32[256,6144]{1,0:T(8,128)} fusion(bf16[256,3072]{1,0:T(8,128)(2,1)S(1)} %bitcast.232, bf16[3072,6144]{1,0:T(8,128)(2,1)} %all-gather.3.cloned.1.call-done), kind=kOutput, calls=%fused_computation.139 | convolution fusion | flops 9663676416 | bytes 45613056 | tf_op jit(solution)/shard_map/dot_general | solution.py:174
  356.5 1.7 slice_bitcast_fusion
  359.4 2.0 fusion.41
  361.4 4.3 all-to-all-start.1
  365.6 2.2 convolution_add_fusion.3
  367.8 1.7 copy.124
  369.6 2.2 multiply_reduce_fusion.2
  371.9 3.0 fusion.42
  374.8 5.2 all-to-all-done.1
  380.0 4.2 all-to-all-start
  384.3 1.8 fusion.66
  386.3 1.3 copy.105
  387.6 10.3 %all-to-all-done = bf16[2,128,16,128]{3,1,0,2:T(8,128)(2,1)} async-done(((bf16[2,128,16,128]{3,1,0,2:T(8,128)(2,1)}), bf16[2,128,16,128]{3,1,0,2:T(8,128)(2,1)}, u32[]{:S(2)}, u32[]{:S(2)}) %all-to-all-start) | async-done | bytes 1048608 | tf_op jit(solution)/shard_map/all_to_all | solution.py:197
  397.9 4.4 all-to-all-start.3
  402.9 1.1 copy.104
  404.0 2.3 copy.100
  406.3 2.3 copy.95
  408.7 6.6 %all-to-all-done.3 = bf16[2,128,16,128]{3,1,0,2:T(8,128)(2,1)} async-done(((bf16[2,128,16,128]{3,1,0,2:T(8,128)(2,1)}), bf16[2,128,16,128]{3,1,0,2:T(8,128)(2,1)}, u32[]{:S(2)}, u32[]{:S(2)}) %all-to-all-start.3) | async-done | bytes 1048608 | tf_op jit(solution)/shard_map/all_to_all | solution.py:199
  415.3 2.3 copy.107
  417.6 51.7 %while.16 = (s32[]{:T(128)}, bf16[8,512,128]{2,1,0:T(8,128)(2,1)}, bf16[8,512,128]{2,1,0:T(8,128)(2,1)}, bf16[8,512,128]{2,1,0:T(8,128)(2,1)}, s32[]{:T(128)}, /...) while((s32[]{:T(128)}, bf16[8,512,128]{2,1,0:T(8,128)(2,1)}, ...), condition=%wide.region_13.14_spmd, body=%wide.region_10.13_spmd.sunk | while | flops 271254016 | bytes 4739165 | solution.py:99
  418.2 1.3 fusion.131
  420.6 1.2 fusion.132
  421.8 2.2 fusion.133
  424.7 1.3 fusion.131
  427.1 1.2 fusion.132
  428.3 2.2 fusion.133
  431.2 1.3 fusion.131
  433.5 1.2 fusion.132
  434.7 2.2 fusion.133
  437.6 1.3 fusion.131
  440.0 1.2 fusion.132
  441.2 2.2 fusion.133
  444.1 1.3 fusion.131
  446.5 1.2 fusion.132
  447.7 2.2 fusion.133
  450.5 1.3 fusion.131
  452.9 1.2 fusion.132
  454.1 2.2 fusion.133
  457.0 1.3 fusion.131
  459.4 1.2 fusion.132
  460.6 2.2 fusion.133
  463.5 1.3 fusion.131
  465.8 1.2 fusion.132
  467.1 2.2 fusion.133
  469.3 2.9 copy.109
  472.2 3.5 all-to-all-start.4
  475.7 2.4 reshape.207
  478.3 10.5 %all-to-all-done.4 = bf16[2,512,4,128]{3,2,0,1:T(4,128)(2,1)S(1)} async-done(((bf16[2,512,4,128]{3,2,0,1:T(4,128)(2,1)}), bf16[2,512,4,128]{3,2,0,1:T(4,128)(2,1)S(1)}, u32[]{:S(2)}, u32[]{:S(2)}) %all-to-all-start.4) | async-done | bytes 1048608 | tf_op jit(solution)/shard_map/all_to_all | solution.py:203
  488.7 1.7 fusion.83
  491.0 1.5 fusion.40
  492.7 4.3 copy.111
  496.9 3.1 reshape.209
  501.6 2.4 fusion.38
  504.0 1.3 fusion.87
  506.6 1.8 convolution_add_fusion.1
  508.5 22.2 %reduce-scatter.5.cloned.1.call-done = f32[128,512]{1,0:T(8,128)} async-done(((f32[128,2048]{1,0:T(8,128)}), f32[128,512]{1,0:T(8,128)}) %reduce-scatter.5.cloned.1.call-update) | async-done | bytes 262160 | tf_op jit(solution)/shard_map/reduce_scatter | solution.py:215
  530.7 36.4 %reduce-scatter.3.cloned.1.call-done = f32[768,128]{1,0:T(8,128)} async-done(((f32[3072,128]{1,0:T(8,128)}), f32[768,128]{1,0:T(8,128)}) %reduce-scatter.3.cloned.1.call-update) | async-done | bytes 393232 | tf_op jit(solution)/shard_map/reduce_scatter | solution.py:214
  567.1 57.6 %all-reduce.3.cloned.1.call-done = (f32[768,128]{1,0:T(8,128)}, f32[128,512]{1,0:T(8,128)}) async-done(((f32[768,128]{1,0:T(8,128)}, f32[128,512]{1,0:T(8,128)}), (f32[768,128]{1,0:T(8,128)}, f32[128,512]{1,0:T(8,128)})) %all-reduce.3.cloned.1.call-update) | async-done | bytes 655376 | tf_op jit(solution)/shard_map/psum | solution.py:212
  624.7 1.8 copy.157
  626.5 1.7 copy.158
  (119 shorter events, 27.4 us)
Async XLA Ops:
  7.2 28.8 %copy-start = (bf16[3072,128]{1,0:T(8,128)(2,1)S(1)}, bf16[3072,128]{1,0:T(8,128)(2,1)}, u32[]{:S(2)}) copy-start(bf16[3072,128]{1,0:T(8,128)(2,1)} %param.26) | copy-start | bytes 2359300
  7.2 0.8 copy-start.16
  7.2 2.2 copy-start.15
  7.2 2.4 copy-start.14
  7.2 2.4 copy-start.12
  7.2 2.4 copy-start.6
  7.2 4.4 copy-start.8
  7.2 330.5 %all-gather.3.cloned.1.call-start = ((), (), s32[]{:S(2)}) async-start(), calls=%async_computation.7 | async-start | bytes 42467328 | tf_op jit(solution)/shard_map/all_gather | solution.py:176
  11.0 2.6 copy-start.13
  11.1 8.7 %collective-permute-start = (bf16[2,64,128]{2,1,0:T(8,128)(2,1)S(1)}, bf16[2,64,128]{2,1,0:T(8,128)(2,1)S(1)}, u32[]{:S(2)}, u32[]{:S(2)}) collective-permute-start(bf16[2,64,128]{2,1,0:T(8,128)(2,1)S(1)} %select_convert_fusion), channel_id=1, source_target_pairs={{0,16},{16,0},{1,17},{17,1},{2,18},{18,2},{3,19},{19,3},{4,20},{20... | collective-permute-start | bytes 98312 | tf_op jit(solution)/shard_map/ppermute | solution.py:23
  12.3 6.2 copy-start.11
  13.6 5.4 copy-start.9
  13.6 20.4 %copy-start.10 = (bf16[64,3072]{1,0:T(8,128)(2,1)S(1)}, bf16[64,3072]{1,0:T(8,128)(2,1)}, u32[]{:S(2)}) copy-start(bf16[64,3072]{1,0:T(8,128)(2,1)} %param.23) | copy-start | bytes 1179652
  13.6 347.8 %all-to-all-start.2 = ((bf16[2,128,16,128]{3,1,0,2:T(8,128)(2,1)}), bf16[2,128,16,128]{3,1,0,2:T(8,128)(2,1)S(1)}, u32[]{:S(2)}, u32[]{:S(2)}) async-start(bf16[2,128,16,128]{3,1,0,2:T(8,128)(2,1)} %copy.102), calls=%async_computation.2 | async-start | bytes 2097152 | tf_op jit(solution)/shard_map/all_to_all | solution.py:200
  35.9 320.6 %copy-start.2 = (bf16[2,128,3072]{2,1,0:T(8,128)(2,1)}, bf16[2,128,3072]{2,1,0:T(8,128)(2,1)S(1)}, u32[]{:S(2)}) copy-start(bf16[2,128,3072]{2,1,0:T(8,128)(2,1)S(1)} %add_convert_fusion) | copy-start | bytes 4718596
  361.4 18.7 %all-to-all-start.1 = ((bf16[2,128,16,128]{3,1,0,2:T(8,128)(2,1)}), bf16[2,128,16,128]{3,1,0,2:T(8,128)(2,1)}, u32[]{:S(2)}, u32[]{:S(2)}) async-start(bf16[2,128,16,128]{3,1,0,2:T(8,128)(2,1)} %fusion.41), calls=%async_computation.1 | async-start | bytes 2097152 | tf_op jit(solution)/shard_map/all_to_all | solution.py:198
  380.0 17.8 %all-to-all-start = ((bf16[2,128,16,128]{3,1,0,2:T(8,128)(2,1)}), bf16[2,128,16,128]{3,1,0,2:T(8,128)(2,1)}, u32[]{:S(2)}, u32[]{:S(2)}) async-start(bf16[2,128,16,128]{3,1,0,2:T(8,128)(2,1)} %fusion.42), calls=%async_computation | async-start | bytes 2097152 | tf_op jit(solution)/shard_map/all_to_all | solution.py:197
  386.3 16.0 %copy-start.17 = (s32[8]{0:T(128)S(1)}, s32[8]{0:T(128)}, u32[]{:S(2)}) copy-start(s32[8]{0:T(128)} %param.20) | copy-start | bytes 100
  397.9 17.4 %all-to-all-start.3 = ((bf16[2,128,16,128]{3,1,0,2:T(8,128)(2,1)}), bf16[2,128,16,128]{3,1,0,2:T(8,128)(2,1)}, u32[]{:S(2)}, u32[]{:S(2)}) async-start(bf16[2,128,16,128]{3,1,0,2:T(8,128)(2,1)} %copy.105), calls=%async_computation.3 | async-start | bytes 2097152 | tf_op jit(solution)/shard_map/all_to_all | solution.py:199
  472.2 16.6 %all-to-all-start.4 = ((bf16[2,512,4,128]{3,2,0,1:T(4,128)(2,1)}), bf16[2,512,4,128]{3,2,0,1:T(4,128)(2,1)S(1)}, u32[]{:S(2)}, u32[]{:S(2)}) async-start(bf16[2,512,4,128]{3,2,0,1:T(4,128)(2,1)} %bitcast.54), calls=%async_computation.4 | async-start | bytes 2097152 | tf_op jit(solution)/shard_map/all_to_all | solution.py:203
  475.7 55.0 %reduce-scatter.5.cloned.1.call-start = ((), (), s32[]{:S(2)}) async-start(), calls=%async_computation.9 | async-start | bytes 1310720 | tf_op jit(solution)/shard_map/reduce_scatter | solution.py:215
  488.7 2.3 copy-start.4
  500.0 1.6 copy-start.5
  504.0 1.4 copy-start.7
  504.0 1.9 copy-start.3
  505.4 61.7 %reduce-scatter.3.cloned.1.call-start = ((), (), s32[]{:S(2)}) async-start(), calls=%async_computation.8 | async-start | bytes 1966080 | tf_op jit(solution)/shard_map/reduce_scatter | solution.py:214
  506.6 121.5 %copy-start.1 = (bf16[3072,128]{1,0:T(8,128)(2,1)S(1)}, bf16[3072,128]{1,0:T(8,128)(2,1)}, u32[]{:S(2)}) copy-start(bf16[3072,128]{1,0:T(8,128)(2,1)} %param.26) | copy-start | bytes 2359300
  508.4 116.2 %all-reduce.3.cloned.1.call-start = ((), (), s32[]{:S(2)}) async-start(), calls=%async_computation.10 | async-start | bytes 1310720 | tf_op jit(solution)/shard_map/psum | solution.py:212
Sparse Core Ops, SparseCore 0:
  9.7 328.0 all-gather.2
  505.5 25.1 reduce-scatter.4
  533.1 33.9 reduce-scatter.2
  570.5 54.1 all-reduce.2
where the time goes:
time: 636 us; the launch traced here: 635 us
  waiting for transfers between devices  451 us (71%)
  matrix products  66.2 us (10%)
  local copies, waits for them, and re-layouts  44.2 us (7%)
  other arithmetic  22.3 us (4%)
  starting transfers between devices  22 us (3%)
  between operations  14.9 us (2%)
  blocking collectives  14.1 us (2%)
    all_gather x1, waiting for transfers between devices, body(): lax.all_gather(frozen_query_key_value, ('pool', 'dp'), axis=0, tiled=True)  301 us
    psum x1, waiting for transfers between devices, body(): summed = lax.psum((grad_down, grad_up), ('pool', 'seq'))  57.6 us
    reduce_scatter x1, waiting for transfers between devices, body(): lax.psum_scatter(summed[0], 'dp', scatter_dimension=0, tiled=True)  36.4 us
    reduce_scatter x1, waiting for transfers between devices, body(): lax.psum_scatter(summed[1], 'dp', scatter_dimension=1, tiled=True)  22.2 us
    dot_general x1, matrix products, body(): jnp.dot(flattened_rows, lax.all_gather(frozen_query_key_value, ('pool', '...  18.7 us
    dot_general x8, matrix products, one_block(): jnp.dot(grad_scores, keys, preferred_element_type=jnp.float32) * factor  17.8 us
    all_gather x1, blocking collectives, body(): spread = lax.all_gather(swapped[None], 'dp', axis=0, tiled=True)  14.1 us
  transfers between devices with their start and end apart: 10, of which 8 were waited for; matrix products, arithmetic and copies ran while one was open for 9% of the time, Pallas kernels for 0%

commit v1 on v0

v1 whole, which is shorter than its diff:
```python
import math

import jax
import jax.numpy as jnp
from jax import lax
from jax.experimental import pallas as pl
from jax.experimental.pallas import tpu as pltpu
from jax.sharding import PartitionSpec as P

HEADS = 16
HEAD_DIM = 128


epsilon = 1e-06
noise_level = 0.5


def partner(block, axis, apart):
    count = lax.axis_size(axis)
    route = []
    for low in range(count):
        high = low | 1 << apart
        if high != low and high < count:
            route += [(low, high), (high, low)]
    return lax.ppermute(block, axis, route)


def norm_rows(values):
    return values * lax.rsqrt(jnp.mean(values * values, -1, keepdims=True) + epsilon)


def layer_norm(values):
    centered = values - jnp.mean(values, -1, keepdims=True)
    return centered * lax.rsqrt(jnp.mean(centered * centered, -1, keepdims=True) + epsilon)


def embed_kernel(kept_ref, inputs_ref, embed_ref, scale_ref, shift_ref, factor_ref, normed_ref, low_ref):
    embedded = lax.dot_general(
        kept_ref[0], embed_ref[...], (((0,), (0,)), ((), ())), preferred_element_type=jnp.float32
    )
    hidden = inputs_ref[...].astype(jnp.float32) + embedded
    normed = (layer_norm(hidden) * (1.0 + scale_ref[0]) + shift_ref[0]).astype(jnp.bfloat16)
    normed_ref[...] = normed
    low_ref[...] = jnp.dot(
        normed, factor_ref[...], preferred_element_type=jnp.float32
    ).astype(jnp.bfloat16)


def embed(kept, inputs, embed_weight, scale, shift, down_factor):
    keep_count, channels, total_rows = kept.shape
    width, rank = down_factor.shape
    block = 128
    blocks = total_rows // block
    whole = lambda *shape: pl.BlockSpec(shape, lambda k, b: (0,) * len(shape))
    one_row = pl.BlockSpec((1, 1, width), lambda k, b: (k, 0, 0))
    out_rows = lambda size: pl.BlockSpec((block, size), lambda k, b: (k * blocks + b, 0))
    return pl.pallas_call(
        embed_kernel,
        grid=(keep_count, blocks),
        in_specs=[
            pl.BlockSpec((1, channels, block), lambda k, b: (k, 0, b)),
            pl.BlockSpec((block, width), lambda k, b: (b, 0)),
            whole(channels, width),
            one_row,
            one_row,
            whole(width, rank),
        ],
        out_specs=[out_rows(width), out_rows(rank)],
        out_shape=[
            jax.ShapeDtypeStruct((keep_count * total_rows, width), jnp.bfloat16),
            jax.ShapeDtypeStruct((keep_count * total_rows, rank), jnp.bfloat16),
        ],
        compiler_params=pltpu.CompilerParams(vmem_limit_bytes=32 * 1024 * 1024),
        cost_estimate=pl.CostEstimate(
            flops=2 * keep_count * total_rows * width * (rank + channels),
            bytes_accessed=keep_count * total_rows * width * 4,
            transcendentals=0,
        ),
    )(kept, inputs, embed_weight, scale[:, None, :], shift[:, None, :], down_factor)


def attend_kernel(length_ref, q_ref, k_ref, v_ref, g_ref, low_ref, up_ref, dlow_ref, gup_ref):
    sample, head = pl.program_id(0), pl.program_id(1)
    total_rows = q_ref.shape[0]
    block_rows = min(512, total_rows)
    length = length_ref[0]
    factor = HEAD_DIM ** (-0.5)
    along = (((1,), (1,)), ((), ()))
    key_raw = k_ref[...]
    keys = norm_rows(key_raw).astype(jnp.bfloat16)
    values = v_ref[...].astype(jnp.bfloat16)
    up = up_ref[...]
    key_mask = lax.broadcasted_iota(jnp.int32, (1, total_rows), 1) < length
    for begin in range(0, total_rows, block_rows):
        rows = pl.ds(begin, block_rows)
        low = low_ref[rows, :]
        query = q_ref[rows, :] + jnp.dot(low, up, preferred_element_type=jnp.float32)
        inverse = lax.rsqrt(jnp.mean(query * query, -1, keepdims=True) + epsilon)
        normal = query * inverse
        row_mask = begin + lax.broadcasted_iota(jnp.int32, (block_rows, 1), 0) < length
        grad = jnp.where(row_mask, g_ref[0, rows, :].astype(jnp.float32), 0.0)
        grad_bf = grad.astype(jnp.bfloat16)
        scores = lax.dot_general(
            normal.astype(jnp.bfloat16), keys, along, preferred_element_type=jnp.float32
        )
        weights = jnp.where(key_mask, jnp.exp2(scores * (factor * math.log2(math.e))), 0.0)
        share = 1.0 / jnp.sum(weights, -1, keepdims=True)
        output = jnp.dot(
            weights.astype(jnp.bfloat16), values, preferred_element_type=jnp.float32
        )
        delta = jnp.sum(grad * output, -1, keepdims=True) * share
        grad_probs = lax.dot_general(
            grad_bf, values, along, preferred_element_type=jnp.float32
        )
        grad_scores = (weights * (grad_probs - delta)).astype(jnp.bfloat16)
        gradient = jnp.dot(grad_scores, keys, preferred_element_type=jnp.float32) * (share * factor)
        inner_mean = jnp.mean(gradient * normal, -1, keepdims=True)
        dquery = (inverse * (gradient - normal * inner_mean)).astype(jnp.bfloat16)
        part = lax.dot_general(dquery, up, along, preferred_element_type=jnp.float32)
        up_part = lax.dot_general(
            dquery, low, (((0,), (0,)), ((), ())), preferred_element_type=jnp.float32
        )

        @pl.when(head == 0)
        def _():
            dlow_ref[rows, :] = part

        @pl.when(head != 0)
        def _():
            dlow_ref[rows, :] += part

        place = pl.ds(pl.multiple_of(head * HEAD_DIM, HEAD_DIM), HEAD_DIM)

        @pl.when(jnp.logical_and(sample == 0, begin == 0))
        def _():
            gup_ref[place, :] = up_part

        @pl.when(jnp.logical_or(sample != 0, begin != 0))
        def _():
            gup_ref[place, :] += up_part


def attend(length, projected, grads, low, up):
    keep_count, total_rows, columns = grads.shape
    heads = columns // HEAD_DIM
    rank = up.shape[0]

    def column_block(first):
        return pl.BlockSpec((total_rows, HEAD_DIM), lambda k, h: (k, first + h))

    return pl.pallas_call(
        attend_kernel,
        grid=(keep_count, heads),
        in_specs=[
            pl.BlockSpec(memory_space=pltpu.SMEM),
            column_block(0),
            column_block(heads),
            column_block(2 * heads),
            pl.BlockSpec((1, total_rows, HEAD_DIM), lambda k, h: (k, 0, h)),
            pl.BlockSpec((total_rows, rank), lambda k, h: (k, 0)),
            pl.BlockSpec((rank, HEAD_DIM), lambda k, h: (0, h)),
        ],
        out_specs=[
            pl.BlockSpec((total_rows, rank), lambda k, h: (k, 0)),
            pl.BlockSpec((columns, rank), lambda k, h: (0, 0)),
        ],
        out_shape=[
            jax.ShapeDtypeStruct((keep_count * total_rows, rank), jnp.float32),
            jax.ShapeDtypeStruct((columns, rank), jnp.float32),
        ],
        compiler_params=pltpu.CompilerParams(vmem_limit_bytes=48 * 1024 * 1024),
    )(length, projected, projected, projected, grads, low, up)


def reduce_kernel(
    sizes, src_ref, down_ref, up_ref, in1, out2, in2, in3, send1, recv1, send2, recv2, send3, recv3
):
    pools, seqs, dps, rows, up_rows = sizes
    plane = pools * seqs
    per = seqs // dps
    wire = in1.dtype
    p, s, d = lax.axis_index("pool"), lax.axis_index("seq"), lax.axis_index("dp")
    me = p * seqs + s
    beside = [lax.rem(me + o, plane) for o in range(1, plane)]
    beside_id = [(j // seqs, lax.rem(j, seqs), d) for j in beside]
    across = [lax.rem(d + o, dps) for o in range(1, dps)]
    across_id = [(p, s, j) for j in across]
    barrier = pltpu.get_barrier_semaphore()
    for target in beside_id + across_id:
        pl.semaphore_signal(barrier, inc=1, device_id=target, device_id_type=pl.DeviceIdType.MESH)
    pl.semaphore_wait(barrier, plane - 1 + dps - 1)

    def copy(src, dst, send, recv, target):
        return pltpu.make_async_remote_copy(
            src_ref=src,
            dst_ref=dst,
            send_sem=send,
            recv_sem=recv,
            device_id=target,
            device_id_type=pl.DeviceIdType.MESH,
        )

    sends = []
    for j, target in zip(beside, beside_id):
        one = copy(src_ref.at[j], in1.at[me], send1.at[j], recv1.at[me], target)
        one.start()
        sends.append(one)
    in1[me] = src_ref[me]
    for j, target in zip(beside, beside_id):
        copy(src_ref.at[j], in1.at[j], send1.at[j], recv1.at[j], target).wait_recv()
    split = dps * rows
    total = in1[0, :split, :].astype(jnp.float32)
    for t in range(1, plane):
        total = total + in1[t, :split, :].astype(jnp.float32)
    for block in range(dps):
        ups = None
        for t in range(plane):
            if t % seqs // per == block:
                term = in1[t, split:, :].astype(jnp.float32)
                ups = term if ups is None else ups + term
        out2[block, :rows, :] = total[block * rows : (block + 1) * rows].astype(wire)
        out2[block, rows:, :] = ups.astype(wire)
    for j, target in zip(across, across_id):
        one = copy(out2.at[j], in2.at[d], send2.at[j], recv2.at[d], target)
        one.start()
        sends.append(one)
    in2[d] = out2[d]
    for j, target in zip(across, across_id):
        copy(out2.at[j], in2.at[j], send2.at[j], recv2.at[j], target).wait_recv()
    owned = in2[0].astype(jnp.float32)
    for t in range(1, dps):
        owned = owned + in2[t].astype(jnp.float32)
    in3[me] = owned.astype(wire)
    for j, target in zip(beside, beside_id):
        one = copy(in3.at[me], in3.at[me], send3.at[j], recv3.at[me], target)
        one.start()
        sends.append(one)
    for j, target in zip(beside, beside_id):
        copy(in3.at[j], in3.at[j], send3.at[j], recv3.at[j], target).wait_recv()
    for t in range(plane):
        down_ref[t * rows : (t + 1) * rows, :] = in3[t, :rows, :].astype(jnp.float32)
        up_ref[t * up_rows : (t + 1) * up_rows, :] = in3[t, rows:, :].astype(jnp.float32)
    for one in sends:
        one.wait_send()


def reduce_gradients(grad_down, grad_up_rows):
    pools, seqs, dps = (lax.axis_size(axis) for axis in ("pool", "seq", "dp"))
    plane = pools * seqs
    per = seqs // dps
    rank = grad_down.shape[1]
    down_rows = grad_down.shape[0] // dps
    own_up = grad_up_rows.shape[0]
    total_up = own_up * per
    rows, up_rows = down_rows // plane, total_up // plane
    wire = jnp.bfloat16 if rows % 16 == 0 and up_rows % 16 == 0 else jnp.float32
    if per > 1:
        here = lax.rem(lax.axis_index("seq"), per)
        grad_up_rows = lax.dynamic_update_slice_in_dim(
            jnp.zeros((total_up, rank), jnp.float32), grad_up_rows, here * own_up, 0
        )
    pieces = jnp.concatenate(
        [
            jnp.transpose(grad_down.reshape(dps, plane, rows, rank), (1, 0, 2, 3)).reshape(
                plane, dps * rows, rank
            ),
            grad_up_rows.reshape(plane, up_rows, rank),
        ],
        1,
    ).astype(wire)
    vmem = pl.BlockSpec(memory_space=pltpu.VMEM)
    dma = pltpu.SemaphoreType.DMA
    return pl.pallas_call(
        lambda *refs: reduce_kernel((pools, seqs, dps, rows, up_rows), *refs),
        in_specs=[vmem],
        out_specs=[vmem, vmem],
        out_shape=[
            jax.ShapeDtypeStruct((down_rows, rank), jnp.float32),
            jax.ShapeDtypeStruct((total_up, rank), jnp.float32),
        ],
        scratch_shapes=[
            pltpu.VMEM((plane, dps * rows + up_rows, rank), wire),
            pltpu.VMEM((dps, rows + up_rows, rank), wire),
            pltpu.VMEM((dps, rows + up_rows, rank), wire),
            pltpu.VMEM((plane, rows + up_rows, rank), wire),
            dma((plane,)),
            dma((plane,)),
            dma((dps,)),
            dma((dps,)),
            dma((plane,)),
            dma((plane,)),
        ],
        compiler_params=pltpu.CompilerParams(
            collective_id=1, has_side_effects=True, vmem_limit_bytes=48 * 1024 * 1024
        ),
    )(pieces)


def body(
    starting_latents,
    noise,
    velocity_matrix,
    kept_rollout_steps,
    trainer_group_of,
    video_valid_tokens,
    block_input_states,
    upstream,
    patch_embed_weight,
    modulation,
    frozen_query_key_value,
    query_down_factor,
    query_up_factor,
):
    halves = lax.axis_size("pool")
    groups = lax.axis_size("dp")
    half = lax.axis_index("pool")
    group = lax.axis_index("dp")
    videos = halves * groups
    video = half * groups + group
    video_ids = jnp.arange(videos, dtype=jnp.int32)
    steps_total = noise.shape[1]
    step_size = 1.0 / steps_total
    own_steps = jnp.sum(jnp.where((video_ids == video)[:, None], kept_rollout_steps, 0), 0)
    state = starting_latents[0].astype(jnp.float32)
    kept_rows = jnp.zeros((own_steps.shape[0],) + state.shape, jnp.float32)
    for step in range(steps_total):
        drift = jnp.dot(velocity_matrix, state, precision=lax.Precision.HIGHEST)
        state = (
            state
            - step_size * drift
            + noise_level * math.sqrt(step_size) * noise[0, step].astype(jnp.float32)
        )
        kept_rows = jnp.where((own_steps == step + 1)[:, None, None], state[None], kept_rows)
    kept_rows = kept_rows.astype(jnp.bfloat16)
    source_half = 1 - half
    trainer_row = jnp.sum(
        jnp.where(
            (jnp.arange(halves, dtype=jnp.int32) == source_half)[:, None], trainer_group_of, 0
        ),
        0,
    )
    source_group = jnp.sum(jnp.where(trainer_row == group, jnp.arange(groups, dtype=jnp.int32), 0))
    source = source_half * groups + source_group
    seqs = lax.axis_size("seq")
    place = lax.axis_index("seq")
    inner_width = query_up_factor.shape[1]
    columns = inner_width // seqs
    inputs_all = lax.all_gather(block_input_states[0], "seq", axis=0, tiled=True)
    grads_all = lax.all_to_all(upstream[0], "seq", split_axis=2, concat_axis=1, tiled=True)
    weight_rows = frozen_query_key_value.shape[0]
    own_weights = lax.dynamic_slice_in_dim(
        frozen_query_key_value.reshape(weight_rows, 3, inner_width), place * columns, columns, 2
    ).reshape(weight_rows, 3 * columns)
    weights = lax.all_gather(own_weights, ("pool", "dp"), axis=0, tiled=True)
    swapped = partner(kept_rows, "pool", 0)
    spread = lax.all_gather(swapped, ("dp", "seq"), axis=0)
    spread = spread.reshape((groups, seqs) + swapped.shape)
    received = lax.dynamic_index_in_dim(spread, source_group, 0, keepdims=False)
    received = jnp.transpose(received, (1, 2, 0, 3)).reshape(
        swapped.shape[0], swapped.shape[1], seqs * swapped.shape[2]
    )
    train_steps = jnp.sum(jnp.where((video_ids == source)[:, None], kept_rollout_steps, 0), 0)
    token_length = jnp.sum(jnp.where(video_ids == source, video_valid_tokens, 0))
    one_hot = (
        train_steps[:, None] - 1 == jnp.arange(steps_total, dtype=jnp.int32)[None, :]
    ).astype(jnp.float32)
    mod_scale = jnp.dot(one_hot, modulation[0], precision=lax.Precision.HIGHEST)
    mod_shift = jnp.dot(one_hot, modulation[1], precision=lax.Precision.HIGHEST)
    flattened_rows, low = embed(
        received, inputs_all, patch_embed_weight, mod_scale, mod_shift, query_down_factor
    )
    projected = jnp.dot(flattened_rows, weights, preferred_element_type=jnp.float32)
    own_up = lax.dynamic_slice_in_dim(query_up_factor, place * columns, columns, 1)
    gradient_low, grad_up_rows = attend(
        token_length.reshape(1), projected, grads_all, low, own_up
    )
    grad_down = lax.dot_general(
        flattened_rows,
        gradient_low.astype(jnp.bfloat16),
        (((0,), (0,)), ((), ())),
        preferred_element_type=jnp.float32,
    )
    owned_down, owned_up = reduce_gradients(grad_down, grad_up_rows)
    return (owned_down, owned_up.T, state[None])


def solution(mesh):
    return jax.shard_map(
        body,
        mesh=mesh,
        in_specs=(
            P(("pool", "dp"), None, "seq"),
            P(("pool", "dp"), None, None, "seq"),
            P(),
            P(),
            P(),
            P(),
            P(("pool", "dp"), "seq", None),
            P(("pool", "dp"), None, "seq", None),
            P(),
            P(),
            P(("pool", "dp"), None),
            P(),
            P(),
        ),
        out_specs=(P("dp", None), P(None, "dp"), P(("pool", "dp"), None, "seq")),
        check_vma=False,
    )
```

time: 636 us -> 228 us (0.36)
  waiting for transfers between devices: 451 us -> 67.6 us
  Pallas kernels: 0 us -> 47.3 us
  matrix products: 66.2 us -> 19.2 us
  blocking collectives: 14.1 us -> 47.8 us
  local copies, waits for them, and re-layouts: 44.2 us -> 21.3 us
  other arithmetic: 22.3 us -> 1.7 us
  starting transfers between devices: 22 us -> 5.34 us
    all_gather x1 -> x2, waiting for transfers between devices: 301 us -> 66.9 us  [the longest x1 66.9 us: body(): weights = lax.all_gather(own_weights, ('pool', 'dp'), axis=0, tiled=True)]
    reduce_scatter x2 -> x0, waiting for transfers between devices: 58.6 us -> none  [the longest x1 36.4 us: body(): lax.psum_scatter(summed[0], 'dp', scatter_dimension=0, tiled=True)]
    psum x1 -> x0, waiting for transfers between devices: 57.6 us -> none  [body(): summed = lax.psum((grad_down, grad_up), ('pool', 'seq'))]
    pallas_call x0 -> x3, Pallas kernels: none -> 47.3 us  [the longest x1 24.2 us: reduce_gradients(): pl.pallas_call(lambda *refs: reduce_kernel((pools, seqs, dps, rows, up_ro...]
    dot_general x32 -> x2, matrix products: 64.4 us -> 17.4 us  [the longest x1 15.5 us: body(): jnp.dot(flattened_rows, weights, preferred_element_type=jnp.float32)]
    all_gather x1, blocking collectives: 14.1 us -> 47.8 us  [body(): spread = lax.all_gather(swapped, ('dp', 'seq'), axis=0)]
    all_to_all x5 -> x1, waiting for transfers between devices: 32.6 us -> 0.01 us  [body(): lax.all_to_all(upstream[0], 'seq', split_axis=2, concat_axis=1, tiled=True)]
    all_to_all x5 -> x1, starting transfers between devices: 21.3 us -> 4.74 us  [body(): lax.all_to_all(upstream[0], 'seq', split_axis=2, concat_axis=1, tiled=True)]
  transfers between devices with their start and end apart: 10 -> 4, of which waited for: 8 -> 1; matrix products, arithmetic and copies ran while one was open for 9% -> 8% of each run, Pallas kernels for 0% -> 4%
where the time goes in v1:
time: 228 us; the launch traced here: 227 us
  waiting for transfers between devices  67.6 us (30%)
  blocking collectives  47.8 us (21%)
  Pallas kernels  47.3 us (21%)
  local copies, waits for them, and re-layouts  21.3 us (9%)
  matrix products  19.2 us (8%)
  between operations  17 us (7%)
  starting transfers between devices  5.34 us (2%)
    all_gather x1, waiting for transfers between devices, body(): weights = lax.all_gather(own_weights, ('pool', 'dp'), axis=0, tiled=True)  66.9 us
    all_gather x1, blocking collectives, body(): spread = lax.all_gather(swapped, ('dp', 'seq'), axis=0)  47.8 us
    pallas_call x1, Pallas kernels, reduce_gradients(): pl.pallas_call(lambda *refs: reduce_kernel((pools, seqs, dps, rows, up_ro...  24.2 us
    unnamed x36, local copies, waits for them, and re-layouts  16.1 us
    dot_general x1, matrix products, body(): jnp.dot(flattened_rows, weights, preferred_element_type=jnp.float32)  15.5 us
    pallas_call x1, Pallas kernels, attend(): pl.pallas_call(attend_kernel, grid=(keep_count, heads), in_specs=[pl.Bloc...  13.9 us
    pallas_call x1, Pallas kernels, embed(): pl.pallas_call(embed_kernel, grid=(keep_count, blocks), in_specs=[pl.Bloc...  9.18 us
    all_to_all x1, starting transfers between devices, body(): lax.all_to_all(upstream[0], 'seq', split_axis=2, concat_axis=1, tiled=True)  4.74 us
  transfers between devices with their start and end apart: 4, of which 1 were waited for; matrix products, arithmetic and copies ran while one was open for 8% of the time, Pallas kernels for 4%

profile of v1, /device:TPU:0, one launch (start us, length us, event | category | flops | bytes accessed | tf_op | source)
XLA Modules:
  0.0 227.2 jit_solution(3668520471869008255)
XLA Ops:
  7.2 0.0 copy-start
  7.2 0.0 all-gather.7.cloned.1.call-start
  7.2 0.7 all-gather.7.cloned.1.call-update
  7.9 0.0 all-gather.5.cloned.1.call-start
  8.0 0.0 copy-start.14
  8.0 0.0 copy-start.13
  8.0 0.0 copy-start.7
  8.0 0.0 copy-start.10
  8.0 0.0 copy-start.12
  8.0 0.0 copy-start.8
  8.0 6.7 %copy.29 = bf16[384,6144]{0,1:T(8,128)(2,1)} copy(bf16[384,6144]{1,0:T(8,128)(2,1)} %param.23) | data formatting | bytes 9437184 | tf_op args[10]
  14.8 2.5 %constant_dynamic-slice_fusion.1 = bf16[384,3,512]{0,2,1:T(8,128)(2,1)} fusion(bf16[384,3,2048]{0,2,1:T(8,128)(2,1)} %bitcast.113, s32[]{:T(128)S(6)} %select_n.66), kind=kLoop, calls=%fused_computation.50 | loop fusion | bytes 2359300 | tf_op jit(solution)/shard_map/dynamic_slice | solution.py:351
  17.3 0.0 all-gather.5.cloned.1.call-update
  17.4 0.0 copy-done.14
  17.4 0.1 select_reduce_fusion.1
  17.4 0.6 fusion.31
  18.8 0.0 copy-done.13
  18.8 0.1 select_reduce_fusion
  18.9 0.0 copy-done.7
  18.9 0.0 copy-done.10
  18.9 0.0 copy-done.12
  19.0 0.1 fusion.22
  19.1 0.2 fusion.20
  19.3 0.2 fusion.17
  19.5 0.2 fusion.14
  19.6 0.2 fusion.11
  19.8 0.2 fusion.8
  20.0 0.2 fusion.5
  20.1 0.2 fusion.2
  20.3 0.0 copy-start.11
  20.3 0.1 select_convert_fusion
  20.4 0.5 collective-permute-start
  21.0 0.0 copy-done.8
  21.0 2.0 copy.30
  23.0 4.7 %all-to-all-start = ((bf16[2,128,2048]{1,0,2:T(2,128)(2,1)}), bf16[2,128,2048]{1,0,2:T(2,128)(2,1)S(1)}, u32[]{:S(2)}, u32[]{:S(2)}) async-start(bf16[2,128,2048]{1,0,2:T(2,128)(2,1)} %bitcast.117), calls=%async_computation | async-start | bytes 2097152 | tf_op jit(solution)/shard_map/all_to_all | solution.py:349
  27.7 0.0 copy-done.9
  27.7 0.2 fusion.26
  28.0 0.0 copy-done
  28.0 0.2 fusion.24
  28.2 0.0 copy-done.15
  28.2 0.6 select_reduce_fusion.3
  30.9 0.0 collective-permute-done
  30.9 47.8 %all-gather = bf16[32,64,128]{2,1,0:T(8,128)(2,1)S(1)} all-gather(bf16[2,64,128]{2,1,0:T(8,128)(2,1)S(1)} %collective-permute-done), channel_id=2, replica_groups=mesh['pool'=2,'seq'=4,'dp'=4] {'dp','seq'}, dimensions={0}, use_global_device_ids=true | all-gather | bytes 557056 | tf_op jit(solution)/shard_map/all_gather | solution.py:356
  78.7 0.0 all-to-all-done
  78.8 0.0 copy-start.6
  78.8 1.0 copy-done.6
  79.8 2.5 %copy.31 = bf16[2,128,4,512]{3,1,2,0:T(8,128)(2,1)S(1)} copy(bf16[2,128,4,512]{1,0,3,2:T(2,128)(2,1)} %bitcast.116) | data formatting | bytes 2097152 | tf_op jit(solution)/shard_map/all_to_all | solution.py:349
  82.3 0.0 all-gather.7.cloned.1.call-done
  82.3 0.0 copy-done.4
  82.4 0.0 copy-done.5
  82.4 0.0 copy-start.3
  82.4 2.0 copy-done.3
  84.4 9.2 %shard_map.148 = (bf16[1024,3072]{1,0:T(8,128)(2,1)S(1)}, bf16[1024,128]{1,0:T(8,128)(2,1)S(1)}) custom-call(bf16[2,64,512]{2,1,0:T(8,128)(2,1)S(1)} %copy_bitcast_fusion.kept_ref, bf16[512,3072]{1,0:T(8,128)(2,1)S(1)} %bitcast.111, bf16[64,3072]{1,0:T(8,128)(2,1)S(1)} %copy-done.5, f32[2,1,3072]{2,1,0:T(1,128)S(1)} %broadcast_in_dim.180.scale_ref, ...), custom_call_target="tpu_custom_call" | custom-call | flops 1207959552 | bytes 12582912 | tf_op jit(solution)/shard_map/pallas_call | solution.py:57
  93.6 2.7 %copy-done.1 = bf16[1024,3072]{1,0:T(8,128)(2,1)} copy-done((bf16[1024,3072]{1,0:T(8,128)(2,1)}, bf16[1024,3072]{1,0:T(8,128)(2,1)S(1)}, u32[]{:S(2)}) %copy-start.1) | copy-done | bytes 6291480
  96.3 66.9 %all-gather.5.cloned.1.call-done = bf16[3072,1536]{0,1:T(8,128)(2,1)} async-done(((bf16[384,1536]{0,1:T(8,128)(2,1)}), bf16[3072,1536]{0,1:T(8,128)(2,1)}) %all-gather.5.cloned.1.call-update) | async-done | bytes 9437200 | tf_op jit(solution)/shard_map/all_gather | solution.py:354
  163.2 15.5 %fusion.34.q_ref.k_ref.v_ref = f32[1024,1536]{1,0:T(8,128)} fusion(bf16[1024,3072]{1,0:T(8,128)(2,1)} %copy-done.1, bf16[3072,1536]{0,1:T(8,128)(2,1)} %all-gather.5.cloned.1.call-done), kind=kOutput, calls=%fused_computation.67 | convolution fusion | flops 9663676416 | bytes 22020096 | tf_op jit(solution)/shard_map/dot_general | solution.py:372
  178.7 13.9 %shard_map.149 = (f32[1024,128]{1,0:T(8,128)S(1)}, f32[512,128]{1,0:T(8,128)S(1)}) custom-call(s32[1]{0:T(128)} %bitcast.22.length_ref, f32[1024,1536]{1,0:T(8,128)} %fusion.34.q_ref.k_ref.v_ref, f32[1024,1536]{1,0:T(8,128)} %fusion.34.q_ref.k_ref.v_ref, f32[1024,1536]{1,0:T(8,128)} %fusion.34.q_ref.k_ref.v_ref, bf16[2,512,512]{2,1,0:T(8,128)(2,1)S(1)} %bitcast.110, ...), custom_call_target="tpu_custom_call" | custom-call | tf_op jit(solution)/shard_map/pallas_call | solution.py:151
  192.6 0.0 copy-done.2
  192.6 1.9 convolution_convert_fusion
  194.5 0.1 copy.32
  194.6 0.1 pad_maximum_fusion.refs_0_
  194.6 24.2 %shard_map.150 = (f32[768,128]{1,0:T(8,128)S(1)}, f32[512,128]{1,0:T(8,128)S(1)}) custom-call(bf16[8,448,128]{2,1,0:T(8,128)(2,1)S(1)} %pad_maximum_fusion.refs_0_), custom_call_target="tpu_custom_call" | custom-call | tf_op jit(solution)/shard_map/pallas_call | solution.py:273
  218.8 0.8 copy.33
  219.7 0.7 copy.37
  (16 shorter events, 0.1 us)
Async XLA Ops:
  7.2 20.8 %copy-start = (bf16[128,2048]{1,0:T(8,128)(2,1)S(1)}, bf16[128,2048]{1,0:T(8,128)(2,1)}, u32[]{:S(2)}) copy-start(bf16[128,2048]{1,0:T(8,128)(2,1)} %param.25) | copy-start | bytes 1572868
  7.2 75.2 %all-gather.7.cloned.1.call-start = ((), (), s32[]{:S(2)}) async-start(), calls=%async_computation.2 | async-start | bytes 3932160 | tf_op jit(solution)/shard_map/all_gather | solution.py:348
  7.9 155.3 %all-gather.5.cloned.1.call-start = ((), (), s32[]{:S(2)}) async-start(), calls=%async_computation.1 | async-start | bytes 10616832 | tf_op jit(solution)/shard_map/all_gather | solution.py:354
  8.0 9.4 %copy-start.14 = (s32[2,4]{1,0:T(2,128)S(1)}, s32[2,4]{1,0:T(2,128)}, u32[]{:S(2)}) copy-start(s32[2,4]{1,0:T(2,128)} %param.17) | copy-start | bytes 100
  8.0 10.8 %copy-start.13 = (s32[8,2]{0,1:T(2,128)S(1)}, s32[8,2]{0,1:T(2,128)}, u32[]{:S(2)}) copy-start(s32[8,2]{0,1:T(2,128)} %param.16) | copy-start | bytes 196
  8.0 10.9 %copy-start.7 = (f32[64,64]{1,0:T(8,128)S(1)}, f32[64,64]{1,0:T(8,128)}, u32[]{:S(2)}) copy-start(f32[64,64]{1,0:T(8,128)} %param.15) | copy-start | bytes 49156
  8.0 10.9 %copy-start.10 = (bf16[1,8,64,128]{3,2,1,0:T(8,128)(2,1)S(1)}, bf16[1,8,64,128]{3,2,1,0:T(8,128)(2,1)}, u32[]{:S(2)}) copy-start(bf16[1,8,64,128]{3,2,1,0:T(8,128)(2,1)} %param.14) | copy-start | bytes 393220
  8.0 10.9 %copy-start.12 = (bf16[1,64,128]{2,1,0:T(8,128)(2,1)S(1)}, bf16[1,64,128]{2,1,0:T(8,128)(2,1)}, u32[]{:S(2)}) copy-start(bf16[1,64,128]{2,1,0:T(8,128)(2,1)} %param.13) | copy-start | bytes 49156
  8.0 12.9 %copy-start.8 = (bf16[1,2,128,2048]{3,2,1,0:T(8,128)(2,1)S(1)}, bf16[1,2,128,2048]{3,2,1,0:T(8,128)(2,1)}, u32[]{:S(2)}) copy-start(bf16[1,2,128,2048]{3,2,1,0:T(8,128)(2,1)} %param.20) | copy-start | bytes 3145732
  14.8 13.0 %copy-start.9 = (f32[2,8,3072]{2,1,0:T(8,128)S(1)}, f32[2,8,3072]{2,1,0:T(8,128)}, u32[]{:S(2)}) copy-start(f32[2,8,3072]{2,1,0:T(8,128)} %param.22) | copy-start | bytes 589828
  14.8 13.5 %copy-start.15 = (s32[8]{0:T(128)S(1)}, s32[8]{0:T(128)}, u32[]{:S(2)}) copy-start(s32[8]{0:T(128)} %param.18) | copy-start | bytes 100
  14.8 67.6 %copy-start.4 = (bf16[3072,128]{1,0:T(8,128)(2,1)S(1)}, bf16[3072,128]{1,0:T(8,128)(2,1)}, u32[]{:S(2)}) copy-start(bf16[3072,128]{1,0:T(8,128)(2,1)} %factor_ref.1) | copy-start | bytes 2359300
  14.8 67.6 %copy-start.5 = (bf16[64,3072]{1,0:T(8,128)(2,1)S(1)}, bf16[64,3072]{1,0:T(8,128)(2,1)}, u32[]{:S(2)}) copy-start(bf16[64,3072]{1,0:T(8,128)(2,1)} %embed_ref.1) | copy-start | bytes 1179652
  20.3 158.4 %copy-start.11 = (f32[64,128]{1,0:T(8,128)}, f32[64,128]{1,0:T(8,128)S(1)}, u32[]{:S(2)}) copy-start(f32[64,128]{1,0:T(8,128)S(1)} %fusion.2) | copy-start | bytes 98308
  20.4 10.4 %collective-permute-start = (bf16[2,64,128]{2,1,0:T(8,128)(2,1)S(1)}, bf16[2,64,128]{2,1,0:T(8,128)(2,1)S(1)}, u32[]{:S(2)}, u32[]{:S(2)}) collective-permute-start(bf16[2,64,128]{2,1,0:T(8,128)(2,1)S(1)} %select_convert_fusion), channel_id=1, source_target_pairs={{0,16},{16,0},{1,17},{17,1},{2,18},{18,2},{3,19},{19,3},{4,20},{20... | collective-permute-start | bytes 98312 | tf_op jit(solution)/shard_map/ppermute | solution.py:25
  23.0 55.8 %all-to-all-start = ((bf16[2,128,2048]{1,0,2:T(2,128)(2,1)}), bf16[2,128,2048]{1,0,2:T(2,128)(2,1)S(1)}, u32[]{:S(2)}, u32[]{:S(2)}) async-start(bf16[2,128,2048]{1,0,2:T(2,128)(2,1)} %bitcast.117), calls=%async_computation | async-start | bytes 2097152 | tf_op jit(solution)/shard_map/all_to_all | solution.py:349
  78.8 1.0 copy-start.6
  82.4 2.0 copy-start.3
  93.6 2.7 %copy-start.1 = (bf16[1024,3072]{1,0:T(8,128)(2,1)}, bf16[1024,3072]{1,0:T(8,128)(2,1)S(1)}, u32[]{:S(2)}) copy-start(bf16[1024,3072]{1,0:T(8,128)(2,1)S(1)} %get-tuple-element.9) | copy-start | bytes 18874372
  178.7 13.9 %copy-start.2 = (bf16[1024,3072]{1,0:T(8,128)(2,1)S(1)}, bf16[1024,3072]{1,0:T(8,128)(2,1)}, u32[]{:S(2)}) copy-start(bf16[1024,3072]{1,0:T(8,128)(2,1)} %copy-done.1) | copy-start | bytes 18874372
Sparse Core Ops, SparseCore 0:
  9.9 60.4 all-gather.6
  71.9 91.1 all-gather.4

commit v2 on v1

--- a/solution.py
+++ b/solution.py
@@ -296,7 +296,7 @@
     )(pieces)
 
 
-def body(
+def body_streamed(
     starting_latents,
     noise,
     velocity_matrix,
@@ -384,7 +384,347 @@
     return (owned_down, owned_up.T, state[None])
 
 
+def attend_slot(query, key_raw, values, grad, low, up, length):
+    factor = HEAD_DIM ** (-0.5)
+    along = (((1,), (1,)), ((), ()))
+    total_rows = query.shape[0]
+    keys = norm_rows(key_raw).astype(jnp.bfloat16)
+    key_mask = lax.broadcasted_iota(jnp.int32, (1, total_rows), 1) < length
+    row_mask = lax.broadcasted_iota(jnp.int32, (total_rows, 1), 0) < length
+    inverse = lax.rsqrt(jnp.mean(query * query, -1, keepdims=True) + epsilon)
+    normal = query * inverse
+    grad = jnp.where(row_mask, grad.astype(jnp.float32), 0.0)
+    scores = lax.dot_general(
+        normal.astype(jnp.bfloat16), keys, along, preferred_element_type=jnp.float32
+    )
+    weights = jnp.where(key_mask, jnp.exp2(scores * (factor * math.log2(math.e))), 0.0)
+    share = 1.0 / jnp.sum(weights, -1, keepdims=True)
+    output = jnp.dot(weights.astype(jnp.bfloat16), values, preferred_element_type=jnp.float32)
+    delta = jnp.sum(grad * output, -1, keepdims=True) * share
+    grad_probs = lax.dot_general(
+        grad.astype(jnp.bfloat16), values, along, preferred_element_type=jnp.float32
+    )
+    grad_scores = (weights * (grad_probs - delta)).astype(jnp.bfloat16)
+    gradient = jnp.dot(grad_scores, keys, preferred_element_type=jnp.float32) * (share * factor)
+    inner_mean = jnp.mean(gradient * normal, -1, keepdims=True)
+    dquery = (inverse * (gradient - normal * inner_mean)).astype(jnp.bfloat16)
+    dlow = lax.dot_general(dquery, up, along, preferred_element_type=jnp.float32)
+    up_rows = lax.dot_general(
+        dquery, low, (((0,), (0,)), ((), ())), preferred_element_type=jnp.float32
+    )
+    return dlow, up_rows
+
+
+def step_kernel(
+    sizes,
+    steps_ref, trainer_ref, tokens_ref, start_ref, noise_ref, velocity_ref, inputs_ref,
+    upstream_ref, embed_ref, modulation_ref, weight_ref, down_ref, up_ref,
+    final_ref, normed_ref, dlow_ref, gup_ref,
+    wall, xall, gall, kall, low_all, projected,
+    local_w, local_x, local_g, send_w, recv_w, send_f, recv_f,
+    send_x, recv_x, send_g, recv_g, send_k, recv_k,
+):
+    pools, seqs, dps = sizes
+    keep_count, tok_rows = kall.shape[2], kall.shape[4]
+    total_rows = seqs * tok_rows
+    weight_rows = weight_ref.shape[0]
+    inner_width = weight_ref.shape[1] // 3
+    heads = wall.shape[0]
+    columns = heads * HEAD_DIM
+    p, s, d = lax.axis_index("pool"), lax.axis_index("seq"), lax.axis_index("dp")
+    other = 1 - p
+    mesh_type = pl.DeviceIdType.MESH
+    seq_peers = [lax.rem(s + o, seqs) for o in range(1, seqs)]
+    dp_peers = [lax.rem(d + o, dps) for o in range(1, dps)]
+    greet = [(p, j, d) for j in seq_peers] + [(p, s, j) for j in dp_peers]
+    greet += [(other, j, i) for i in range(dps) for j in range(seqs)]
+
+    def block_rows(pool, group):
+        return pl.ds(pl.multiple_of((pool * dps + group) * weight_rows, weight_rows), weight_rows)
+
+    own_rows = block_rows(p, d)
+    local = []
+    for h in range(heads):
+        for part in range(3):
+            first = pl.multiple_of(part * inner_width + s * columns + h * HEAD_DIM, HEAD_DIM)
+            local.append(
+                pltpu.make_async_copy(
+                    weight_ref.at[:, pl.ds(first, HEAD_DIM)],
+                    wall.at[h, own_rows, pl.ds(part * HEAD_DIM, HEAD_DIM)],
+                    local_w.at[h, part],
+                )
+            )
+    local_inputs = pltpu.make_async_copy(inputs_ref.at[0], xall.at[s], local_x)
+
+    def grads_of(j):
+        return upstream_ref.at[0, :, :, pl.ds(pl.multiple_of(j * columns, columns), columns)]
+
+    local_grads = pltpu.make_async_copy(grads_of(s), gall.at[s], local_g)
+    for one in local + [local_inputs, local_grads]:
+        one.start()
+    barrier = pltpu.get_barrier_semaphore()
+    for target in greet:
+        pl.semaphore_signal(barrier, inc=1, device_id=target, device_id_type=mesh_type)
+    pl.semaphore_wait(barrier, len(greet))
+
+    def copy(src, dst, send, recv, target):
+        return pltpu.make_async_remote_copy(
+            src_ref=src,
+            dst_ref=dst,
+            send_sem=send,
+            recv_sem=recv,
+            device_id=target,
+            device_id_type=mesh_type,
+        )
+
+    sends = []
+
+    def launch(*args):
+        one = copy(*args)
+        one.start()
+        sends.append(one)
+
+    for one in local[:3]:
+        one.wait()
+    for j in dp_peers:
+        launch(wall.at[0, own_rows], wall.at[0, own_rows], send_w.at[0, j], recv_w.at[0, d], (p, s, j))
+    for j in seq_peers:
+        launch(inputs_ref.at[0], xall.at[s], send_x.at[j], recv_x.at[s], (p, j, d))
+    for one in local[3:]:
+        one.wait()
+    for h in range(1, heads):
+        for j in dp_peers:
+            launch(
+                wall.at[h, own_rows], wall.at[h, own_rows], send_w.at[h, j], recv_w.at[h, d], (p, s, j)
+            )
+    for h in range(heads):
+        launch(
+            wall.at[h, own_rows], wall.at[h, own_rows], send_f.at[h, d], recv_f.at[h, d], (other, s, d)
+        )
+    for j in seq_peers:
+        launch(grads_of(j), gall.at[s], send_g.at[j], recv_g.at[s], (p, j, d))
+
+    video = p * dps + d
+    steps_total = noise_ref.shape[1]
+    step_size = 1.0 / steps_total
+    state = start_ref[0].astype(jnp.float32)
+    velocity = velocity_ref[...]
+    kept_rows = [jnp.zeros_like(state) for _ in range(keep_count)]
+    for step in range(steps_total):
+        drift = jnp.dot(
+            velocity, state, precision=lax.Precision.HIGHEST, preferred_element_type=jnp.float32
+        )
+        state = (
+            state
+            - step_size * drift
+            + noise_level * math.sqrt(step_size) * noise_ref[0, step].astype(jnp.float32)
+        )
+        for k in range(keep_count):
+            kept_rows[k] = jnp.where(steps_ref[video, k] == step + 1, state, kept_rows[k])
+    final_ref[0] = state
+    mine = seqs * dps
+    for k in range(keep_count):
+        kall[mine, 0, k] = kept_rows[k].astype(jnp.bfloat16)
+    for i in range(dps):
+        for j in range(seqs):
+            launch(
+                kall.at[mine, 0],
+                kall.at[d * seqs + s, 0],
+                send_k.at[i * seqs + j],
+                recv_k.at[d * seqs + s],
+                (other, j, i),
+            )
+
+    source_group = jnp.int32(0)
+    for i in range(dps):
+        source_group = jnp.where(trainer_ref[other, i] == d, i, source_group)
+    source = other * dps + source_group
+    length = tokens_ref[source]
+    for i in range(dps):
+        for j in range(seqs):
+            spot = i * seqs + j
+            copy(
+                kall.at[mine, 0], kall.at[spot, 0], send_k.at[spot], recv_k.at[spot], (other, j, i)
+            ).wait_recv()
+    scales, shifts = [], []
+    for k in range(keep_count):
+        wanted = steps_ref[source, k]
+        scale = jnp.zeros((1, normed_ref.shape[1]), jnp.float32)
+        shift = scale
+        for t in range(steps_total):
+            scale = scale + jnp.where(wanted == t + 1, modulation_ref[0, t : t + 1, :], 0.0)
+            shift = shift + jnp.where(wanted == t + 1, modulation_ref[1, t : t + 1, :], 0.0)
+        scales.append(1.0 + scale)
+        shifts.append(shift)
+    local_inputs.wait()
+    embed_weight = embed_ref[...]
+    order = [s] + seq_peers
+    for o, j in enumerate(order):
+        if o > 0:
+            copy(inputs_ref.at[0], xall.at[j], send_x.at[j], recv_x.at[j], (p, j, d)).wait_recv()
+        for k in range(keep_count):
+            kept = jnp.zeros(kall.shape[3:], jnp.float32)
+            for i in range(dps):
+                kept = kept + jnp.where(
+                    source_group == i, kall[i * seqs + j, 0, k].astype(jnp.float32), 0.0
+                )
+            embedded = lax.dot_general(
+                kept.astype(jnp.bfloat16),
+                embed_weight,
+                (((0,), (0,)), ((), ())),
+                preferred_element_type=jnp.float32,
+            )
+            hidden = xall[j].astype(jnp.float32) + embedded
+            normed = (layer_norm(hidden) * scales[k] + shifts[k]).astype(jnp.bfloat16)
+            rows = pl.ds(pl.multiple_of(k * total_rows + j * tok_rows, tok_rows), tok_rows)
+            normed_ref[rows, :] = normed
+            low_all[rows, :] = jnp.dot(
+                normed, down_ref[...], preferred_element_type=jnp.float32
+            ).astype(jnp.bfloat16)
+
+    local_grads.wait()
+    for j in seq_peers:
+        copy(grads_of(j), gall.at[j], send_g.at[j], recv_g.at[j], (p, j, d)).wait_recv()
+    for h in range(heads):
+        for j in dp_peers:
+            there = block_rows(p, j)
+            copy(
+                wall.at[h, there], wall.at[h, there], send_w.at[h, j], recv_w.at[h, j], (p, s, j)
+            ).wait_recv()
+            launch(
+                wall.at[h, there], wall.at[h, there], send_f.at[h, j], recv_f.at[h, j], (other, s, d)
+            )
+        for j in [d] + dp_peers:
+            there = block_rows(other, j)
+            copy(
+                wall.at[h, there], wall.at[h, there], send_f.at[h, j], recv_f.at[h, j], (other, s, d)
+            ).wait_recv()
+        up = up_ref[:, pl.ds(pl.multiple_of(s * columns + h * HEAD_DIM, HEAD_DIM), HEAD_DIM)]
+        gup = None
+        for k in range(keep_count):
+            rows = slice(k * total_rows, (k + 1) * total_rows)
+            projected[...] = jnp.dot(
+                normed_ref[rows, :], wall[h], preferred_element_type=jnp.float32
+            )
+            low = low_all[rows, :]
+            query = projected[:, :HEAD_DIM] + jnp.dot(low, up, preferred_element_type=jnp.float32)
+            grad = gall[:, k, :, h * HEAD_DIM : (h + 1) * HEAD_DIM].reshape(total_rows, HEAD_DIM)
+            dlow, up_rows = attend_slot(
+                query,
+                projected[:, HEAD_DIM : 2 * HEAD_DIM],
+                projected[:, 2 * HEAD_DIM :].astype(jnp.bfloat16),
+                grad,
+                low,
+                up,
+                length,
+            )
+            dlow_ref[rows, :] = dlow if h == 0 else dlow_ref[rows, :] + dlow
+            gup = up_rows if gup is None else gup + up_rows
+        gup_ref[h * HEAD_DIM : (h + 1) * HEAD_DIM, :] = gup
+    for one in sends:
+        one.wait_send()
+
+
+def train_step(*arguments):
+    (
+        steps, trainer, tokens, start, noise, velocity, inputs, upstream, embed_weight,
+        modulation, weight, down, up,
+    ) = arguments
+    pools, seqs, dps = (lax.axis_size(axis) for axis in ("pool", "seq", "dp"))
+    keep_count, tok_rows = upstream.shape[1:3]
+    channels = start.shape[1]
+    width, rank = down.shape
+    inner_width = up.shape[1]
+    columns = inner_width // seqs
+    heads = columns // HEAD_DIM
+    total_rows = seqs * tok_rows
+    vmem = pl.BlockSpec(memory_space=pltpu.VMEM)
+    smem = pl.BlockSpec(memory_space=pltpu.SMEM)
+    hbm = pl.BlockSpec(memory_space=pl.ANY)
+    dma = pltpu.SemaphoreType.DMA
+    bf = jnp.bfloat16
+    return pl.pallas_call(
+        lambda *refs: step_kernel((pools, seqs, dps), *refs),
+        in_specs=[smem] * 3 + [vmem] * 3 + [hbm] * 2 + [vmem] * 2 + [hbm] + [vmem] * 2,
+        out_specs=[vmem] * 4,
+        out_shape=[
+            jax.ShapeDtypeStruct((1, channels, tok_rows), jnp.float32),
+            jax.ShapeDtypeStruct((keep_count * total_rows, width), bf),
+            jax.ShapeDtypeStruct((keep_count * total_rows, rank), jnp.float32),
+            jax.ShapeDtypeStruct((columns, rank), jnp.float32),
+        ],
+        scratch_shapes=[
+            pltpu.VMEM((heads, width, 3 * HEAD_DIM), bf),
+            pltpu.VMEM((seqs, tok_rows, width), bf),
+            pltpu.VMEM((seqs, keep_count, tok_rows, columns), bf),
+            pltpu.VMEM((seqs * dps + 1, 1, keep_count, channels, tok_rows), bf),
+            pltpu.VMEM((keep_count * total_rows, rank), bf),
+            pltpu.VMEM((total_rows, 3 * HEAD_DIM), jnp.float32),
+            dma((heads, 3)),
+            dma,
+            dma,
+            dma((heads, dps)),
+            dma((heads, dps)),
+            dma((heads, dps)),
+            dma((heads, dps)),
+            dma((seqs,)),
+            dma((seqs,)),
+            dma((seqs,)),
+            dma((seqs,)),
+            dma((seqs * dps,)),
+            dma((seqs * dps,)),
+        ],
+        compiler_params=pltpu.CompilerParams(
+            collective_id=2, has_side_effects=True, vmem_limit_bytes=56 * 1024 * 1024
+        ),
+    )(*arguments)
+
+
+def body_in_vmem(
+    starting_latents,
+    noise,
+    velocity_matrix,
+    kept_rollout_steps,
+    trainer_group_of,
+    video_valid_tokens,
+    block_input_states,
+    upstream,
+    patch_embed_weight,
+    modulation,
+    frozen_query_key_value,
+    query_down_factor,
+    query_up_factor,
+):
+    final, normed, gradient_low, grad_up_rows = train_step(
+        kept_rollout_steps,
+        trainer_group_of,
+        video_valid_tokens,
+        starting_latents,
+        noise,
+        velocity_matrix,
+        block_input_states,
+        upstream,
+        patch_embed_weight,
+        modulation,
+        frozen_query_key_value,
+        query_down_factor,
+        query_up_factor,
+    )
+    grad_down = lax.dot_general(
+        normed,
+        gradient_low.astype(jnp.bfloat16),
+        (((0,), (0,)), ((), ())),
+        preferred_element_type=jnp.float32,
+    )
+    owned_down, owned_up = reduce_gradients(grad_down, grad_up_rows)
+    return (owned_down, owned_up.T, final)
+
+
 def solution(mesh):
+    def body(*arguments):
+        tokens = arguments[6].shape[1] * lax.axis_size("seq")
+        return (body_in_vmem if tokens <= 512 else body_streamed)(*arguments)
+
     return jax.shard_map(
         body,
         mesh=mesh,

time: 228 us -> 203 us (0.89)
  Pallas kernels: 47.3 us -> 193 us
  waiting for transfers between devices: 67.6 us -> 0 us
  blocking collectives: 47.8 us -> 0 us
  local copies, waits for them, and re-layouts: 21.3 us -> 3.61 us
  between operations: 17 us -> 0.68 us
  matrix products: 19.2 us -> 4.71 us
  starting transfers between devices: 5.34 us -> 0 us
    pallas_call x2 -> x1, Pallas kernels: 23.1 us -> 164 us  [train_step(): pl.pallas_call(lambda *refs: step_kernel((pools, seqs, dps), *refs), in_s...]
    all_gather x2 -> x0, waiting for transfers between devices: 66.9 us -> none  [the longest x1 66.9 us: body(): weights = lax.all_gather(own_weights, ('pool', 'dp'), axis=0, tiled=True)]
    all_gather x1 -> x0, blocking collectives: 47.8 us -> none  [body(): spread = lax.all_gather(swapped, ('dp', 'seq'), axis=0)]
    dot_general x12 -> x1, matrix products: 19.2 us -> 4.71 us  [body_in_vmem(): lax.dot_general(normed, gradient_low.astype(jnp.bfloat16), (((0,), (0,)),...]
    unnamed x36 -> x6, local copies, waits for them, and re-layouts: 16.1 us -> 3.55 us
    all_to_all x1 -> x0, starting transfers between devices: 4.74 us -> none  [body(): lax.all_to_all(upstream[0], 'seq', split_axis=2, concat_axis=1, tiled=True)]
    pallas_call x1, Pallas kernels: 24.2 us -> 28.6 us  [reduce_gradients(): pl.pallas_call(lambda *refs: reduce_kernel((pools, seqs, dps, rows, up_ro...]
    dynamic_slice x2 -> x0, local copies, waits for them, and re-layouts: 2.54 us -> none  [the longest x1 2.53 us: body(): lax.dynamic_slice_in_dim(frozen_query_key_value.reshape(weight_rows, 3, i...]
  transfers between devices with their start and end apart: 4 -> 0, of which waited for: 1 -> 0; matrix products, arithmetic and copies ran while one was open for 8% -> 0% of each run, Pallas kernels for 4% -> 0%
where the time goes in v2:
time: 203 us
  Pallas kernels  193 us (95%)
  matrix products  4.71 us (2%)
  local copies, waits for them, and re-layouts  3.61 us (2%)
    pallas_call x1, Pallas kernels, train_step(): pl.pallas_call(lambda *refs: step_kernel((pools, seqs, dps), *refs), in_s...  164 us
    pallas_call x1, Pallas kernels, reduce_gradients(): pl.pallas_call(lambda *refs: reduce_kernel((pools, seqs, dps, rows, up_ro...  28.6 us
    dot_general x1, matrix products, body_in_vmem(): lax.dot_general(normed, gradient_low.astype(jnp.bfloat16), (((0,), (0,)),...  4.71 us

profile of v2, /device:TPU:0, one launch (start us, length us, event | category | flops | bytes accessed | tf_op | source)
XLA Modules:
  0.0 202.6 jit_solution(242468663539905392)
XLA Ops:
  0.6 1.3 copy.16.refs_0_
  2.0 164.0 %shard_map.148 = (f32[1,64,128]{2,1,0:T(8,128)}, bf16[1024,3072]{1,0:T(8,128)(2,1)}, f32[1024,128]{1,0:T(8,128)}, f32[512,128]{1,0:T(8,128)}) custom-call(s32[8,2]{1,0:T(8,128)} %copy.16.refs_0_, s32[2,4]{1,0:T(2,128)} %refs_1_.1, s32[8]{0:T(128)} %refs_2_.1, bf16[1,64,128]{2,1,0:T(8,128)(2,1)} %refs_3_.1, bf16[1,8,64,128]{3,2,1,0:T(8,128)(2,1)} %refs_4_.1, ...), custom_call_target="tpu_custom_call" | custom-call | tf_op jit(solution)/shard_map/pallas_call | solution.py:646
  166.0 1.0 convert.11
  167.0 4.7 %convolution_convert_fusion = bf16[3072,128]{1,0:T(8,128)(2,1)S(1)} fusion(bf16[1024,3072]{1,0:T(8,128)(2,1)} %get-tuple-element.9, f32[1024,128]{1,0:T(8,128)} %get-tuple-element.10), kind=kOutput, calls=%fused_computation | convolution fusion | flops 805830656 | bytes 7602176 | tf_op jit(solution)/shard_map/dot_general | solution.py:713
  171.7 0.0 copy-start
  171.7 0.1 copy.17
  171.8 0.1 pad_maximum_fusion.refs_0_
  171.8 28.6 %shard_map.149 = (f32[768,128]{1,0:T(8,128)S(1)}, f32[512,128]{1,0:T(8,128)S(1)}) custom-call(bf16[8,448,128]{2,1,0:T(8,128)(2,1)S(1)} %pad_maximum_fusion.refs_0_), custom_call_target="tpu_custom_call" | custom-call | tf_op jit(solution)/shard_map/pallas_call | solution.py:273
  200.4 0.8 copy.18
  201.3 0.7 copy.21
  202.0 0.0 copy-done
  202.0 0.6 copy.22
Async XLA Ops:
  171.7 30.3 %copy-start = (f32[1,64,128]{2,1,0:T(8,128)S(1)}, f32[1,64,128]{2,1,0:T(8,128)}, u32[]{:S(2)}) copy-start(f32[1,64,128]{2,1,0:T(8,128)} %get-tuple-element.23) | copy-start | bytes 98308

commit v3 on v2

--- a/solution.py
+++ b/solution.py
@@ -484,6 +484,37 @@
         one.start()
         sends.append(one)
 
+    video = p * dps + d
+    steps_total = noise_ref.shape[1]
+    step_size = 1.0 / steps_total
+    state = start_ref[0].astype(jnp.float32)
+    velocity = velocity_ref[...]
+    kept_rows = [jnp.zeros_like(state) for _ in range(keep_count)]
+    for step in range(steps_total):
+        drift = jnp.dot(
+            velocity, state, precision=lax.Precision.HIGHEST, preferred_element_type=jnp.float32
+        )
+        state = (
+            state
+            - step_size * drift
+            + noise_level * math.sqrt(step_size) * noise_ref[0, step].astype(jnp.float32)
+        )
+        for k in range(keep_count):
+            kept_rows[k] = jnp.where(steps_ref[video, k] == step + 1, state, kept_rows[k])
+    final_ref[0] = state
+    mine = seqs * dps
+    for k in range(keep_count):
+        kall[mine, 0, k] = kept_rows[k].astype(jnp.bfloat16)
+    for i in range(dps):
+        for j in range(seqs):
+            launch(
+                kall.at[mine, 0],
+                kall.at[d * seqs + s, 0],
+                send_k.at[i * seqs + j],
+                recv_k.at[d * seqs + s],
+                (other, j, i),
+            )
+
     for one in local[:3]:
         one.wait()
     for j in dp_peers:
@@ -503,37 +534,6 @@
         )
     for j in seq_peers:
         launch(grads_of(j), gall.at[s], send_g.at[j], recv_g.at[s], (p, j, d))
-
-    video = p * dps + d
-    steps_total = noise_ref.shape[1]
-    step_size = 1.0 / steps_total
-    state = start_ref[0].astype(jnp.float32)
-    velocity = velocity_ref[...]
-    kept_rows = [jnp.zeros_like(state) for _ in range(keep_count)]
-    for step in range(steps_total):
-        drift = jnp.dot(
-            velocity, state, precision=lax.Precision.HIGHEST, preferred_element_type=jnp.float32
-        )
-        state = (
-            state
-            - step_size * drift
-            + noise_level * math.sqrt(step_size) * noise_ref[0, step].astype(jnp.float32)
-        )
-        for k in range(keep_count):
-            kept_rows[k] = jnp.where(steps_ref[video, k] == step + 1, state, kept_rows[k])
-    final_ref[0] = state
-    mine = seqs * dps
-    for k in range(keep_count):
-        kall[mine, 0, k] = kept_rows[k].astype(jnp.bfloat16)
-    for i in range(dps):
-        for j in range(seqs):
-            launch(
-                kall.at[mine, 0],
-                kall.at[d * seqs + s, 0],
-                send_k.at[i * seqs + j],
-                recv_k.at[d * seqs + s],
-                (other, j, i),
-            )
 
     source_group = jnp.int32(0)
     for i in range(dps):

time: 203 us -> 171 us (0.84)
  Pallas kernels: 193 us -> 160 us
    pallas_call x1, Pallas kernels: 164 us -> 130 us  [train_step(): pl.pallas_call(lambda *refs: step_kernel((pools, seqs, dps), *refs), in_s...]
    pallas_call x1, Pallas kernels: 28.6 us -> 30.8 us  [reduce_gradients(): pl.pallas_call(lambda *refs: reduce_kernel((pools, seqs, dps, rows, up_ro...]
where the time goes in v3:
time: 171 us; the launch traced here: 170 us
  Pallas kernels  160 us (94%)
  matrix products  4.71 us (3%)
  local copies, waits for them, and re-layouts  3.61 us (2%)
    pallas_call x1, Pallas kernels, train_step(): pl.pallas_call(lambda *refs: step_kernel((pools, seqs, dps), *refs), in_s...  130 us
    pallas_call x1, Pallas kernels, reduce_gradients(): pl.pallas_call(lambda *refs: reduce_kernel((pools, seqs, dps, rows, up_ro...  30.8 us
    dot_general x1, matrix products, body_in_vmem(): lax.dot_general(normed, gradient_low.astype(jnp.bfloat16), (((0,), (0,)),...  4.71 us
    unnamed x6, local copies, waits for them, and re-layouts  3.55 us

profile of v3, /device:TPU:0, one launch (start us, length us, event | category | flops | bytes accessed | tf_op | source)
XLA Modules:
  0.0 170.4 jit_solution(5716771257724842077)
XLA Ops:
  0.6 1.3 copy.16.refs_0_
  2.0 129.6 %shard_map.148 = (f32[1,64,128]{2,1,0:T(8,128)}, bf16[1024,3072]{1,0:T(8,128)(2,1)}, f32[1024,128]{1,0:T(8,128)}, f32[512,128]{1,0:T(8,128)}) custom-call(s32[8,2]{1,0:T(8,128)} %copy.16.refs_0_, s32[2,4]{1,0:T(2,128)} %refs_1_.1, s32[8]{0:T(128)} %refs_2_.1, bf16[1,64,128]{2,1,0:T(8,128)(2,1)} %refs_3_.1, bf16[1,8,64,128]{3,2,1,0:T(8,128)(2,1)} %refs_4_.1, ...), custom_call_target="tpu_custom_call" | custom-call | tf_op jit(solution)/shard_map/pallas_call | solution.py:646
  131.6 1.0 convert.11
  132.6 4.7 %convolution_convert_fusion = bf16[3072,128]{1,0:T(8,128)(2,1)S(1)} fusion(bf16[1024,3072]{1,0:T(8,128)(2,1)} %get-tuple-element.9, f32[1024,128]{1,0:T(8,128)} %get-tuple-element.10), kind=kOutput, calls=%fused_computation | convolution fusion | flops 805830656 | bytes 7602176 | tf_op jit(solution)/shard_map/dot_general | solution.py:713
  137.3 0.0 copy-start
  137.3 0.1 copy.17
  137.4 0.1 pad_maximum_fusion.refs_0_
  137.4 30.8 %shard_map.149 = (f32[768,128]{1,0:T(8,128)S(1)}, f32[512,128]{1,0:T(8,128)S(1)}) custom-call(bf16[8,448,128]{2,1,0:T(8,128)(2,1)S(1)} %pad_maximum_fusion.refs_0_), custom_call_target="tpu_custom_call" | custom-call | tf_op jit(solution)/shard_map/pallas_call | solution.py:273
  168.2 0.8 copy.18
  169.0 0.7 copy.21
  169.8 0.0 copy-done
  169.8 0.6 copy.22
Async XLA Ops:
  137.3 32.5 %copy-start = (f32[1,64,128]{2,1,0:T(8,128)S(1)}, f32[1,64,128]{2,1,0:T(8,128)}, u32[]{:S(2)}) copy-start(f32[1,64,128]{2,1,0:T(8,128)} %get-tuple-element.23) | copy-start | bytes 98308
